TPU v7x, 768 devices: a whole 4x8x12 slice. The times are simulated.
768 devices in a mesh: index: 24 (over x, z_hi, core), ingest: 32 (over y, z_lo).
Axes of the slice: x: 4, y: 8, z: 12 (z_hi: 3, z_lo: 4; z = z_hi * 4 + z_lo), core: 2. Of those that a mesh axis runs over, the one named last changes fastest.
Arguments:
- vectors: bfloat16 [98304, 768], P(('index', 'ingest')), may hold values from -6 to 6
- rotation: bfloat16 [768, 768], replicated, may hold values from -0.21875 to 0.21875
- centroids: bfloat16 [2048, 768], P('ingest'), may hold values from -6 to 6
- assignment: int32 [98304], P(('index', 'ingest')), may hold values from 0 to 2047
- block_order: int32 [24, 32], P('index'), may hold values from 0 to 31, each once within a row
- destination: int32 [24, 32, 1], P('index'), may hold values from 0 to 23; in each aligned block of 32 rows (0 to 31, 32 to 63, ..., all dimensions but the last counted through in order) at most 3 rows name the same one
- live_count: int32 [24], P('index'), may hold values from 24 to 32
Outputs:
- rebalanced: bfloat16 [768, 221184], P('ingest', 'index')
Inputs may be any that keep to these rules, and one draw needn't show every extreme that they name: In each owner's list of 32 entries no destination is named by more than 3 entries. `block_order`: each owner's list names each of its 32 blocks once.
All inputs are finite; a program needn't handle non-finite values.
Results may differ from a plain program's by a relative error of at most 0.01.
Values may be sent and summed in bfloat16 or wider, within the bound.
A program may use at most 32 MiB of HBM per device.

v0:
```python
import jax
import jax.numpy as jnp
from jax import lax
from jax.sharding import PartitionSpec as P

BROWS = 128


def turn_rows(rotation, rows):
    return lax.dot_general(
        rotation, rows, (((0,), (1,)), ((), ())), preferred_element_type=jnp.float32
    ).astype(jnp.bfloat16)


def body(vectors, rotation, centroids, assignment, block_order, destination, live_count):
    rotated = turn_rows(rotation, vectors)
    piece = lax.all_gather(centroids, "ingest", axis=0, tiled=True)
    turned = turn_rows(rotation, piece)
    width = piece.shape[0]
    valid = (assignment >= 0) & (assignment < width)
    taken = jnp.take(turned, jnp.clip(assignment, 0, width - 1), axis=1)
    looked = jnp.where(valid[None, :], taken.astype(jnp.float32), 0.0)
    residual = (rotated.astype(jnp.float32) - looked).astype(jnp.bfloat16)
    grouped = lax.all_to_all(residual, "ingest", split_axis=0, concat_axis=1, tiled=True)
    owners = lax.axis_size("index")
    feature_rows = grouped.shape[0]
    blocks = grouped.shape[1] // BROWS
    capacity = max(2, 2 * blocks // owners + 1)
    entry = jnp.arange(blocks, dtype=jnp.int32)
    live = entry < live_count[0]
    dest = destination[0, :, 0]
    hits = ((dest[:, None] == jnp.arange(owners, dtype=jnp.int32)[None, :]) & live[:, None]).astype(
        jnp.int32
    )
    before = jnp.cumsum(hits, axis=0) - hits
    slot = jnp.sum(before * hits, axis=1)
    picked_mask = block_order[0][:, None] == entry[None, :]
    live_dest = jnp.where(live, dest, owners)
    block_dest = jnp.sum(jnp.where(picked_mask, live_dest[:, None], 0), axis=0)
    block_slot = jnp.sum(jnp.where(picked_mask, slot[:, None], 0), axis=0)
    here = lax.axis_index("index")
    slot_ids = jnp.arange(capacity, dtype=jnp.int32)
    slabs = lax.all_gather(grouped[None], "index", axis=0, tiled=True)
    dests = lax.all_gather(block_dest.astype(jnp.bfloat16)[None], "index", axis=0, tiled=True)
    slots = lax.all_gather(block_slot.astype(jnp.bfloat16)[None], "index", axis=0, tiled=True)
    count = slabs.shape[0]
    wanted = dests.astype(jnp.int32) == here
    match = slots.astype(jnp.int32)[:, None, :] == slot_ids[None, :, None]
    select = (wanted[:, None, :] & match).astype(jnp.bfloat16)
    tiles = slabs.reshape(count, feature_rows, blocks, BROWS)
    placed = jnp.einsum("kcb,kfbr->fkcr", select, tiles, preferred_element_type=jnp.float32).astype(
        jnp.bfloat16
    )
    return placed.reshape(feature_rows, owners * capacity * BROWS)


def solution(mesh):
    return jax.shard_map(
        body,
        mesh=mesh,
        in_specs=(
            P(("index", "ingest"), None),
            P(),
            P("ingest", None),
            P(("index", "ingest")),
            P("index", None),
            P("index", None, None),
            P("index"),
        ),
        out_specs=P("ingest", "index"),
        check_vma=False,
    )
```

profile of v0, /device:TPU:1, one launch (start us, length us, event | category | flops | bytes accessed | tf_op | source)
XLA Modules:
  0.0 321.2 jit_solution(14211525172785021487)
XLA Ops:
  6.5 0.0 copy-start
  6.5 0.0 all-gather.5.cloned.1.call-start
  6.5 0.7 all-gather.5.cloned.1.call-update
  7.3 0.0 all-gather.7.cloned.1.call-start
  7.3 0.7 compare_and_fusion
  8.0 155.2 %all-gather.5.cloned.1.call-done = bf16[2048,768]{1,0:T(8,128)(2,1)} async-done(((bf16[64,768]{1,0:T(8,128)(2,1)}), bf16[2048,768]{1,0:T(8,128)(2,1)}) %all-gather.5.cloned.1.call-update) | async-done | bytes 3145744 | tf_op jit(solution)/shard_map/all_gather | solution.py:17
  163.2 0.0 copy-done
  163.2 6.0 %convolution_convert_fusion = bf16[768,2048]{1,0:T(8,128)(2,1)} fusion(bf16[768,768]{1,0:T(8,128)(2,1)S(1)} %copy-done, bf16[2048,768]{1,0:T(8,128)(2,1)} %all-gather.5.cloned.1.call-done), kind=kOutput, calls=%fused_computation.3 | convolution fusion | flops 2417491968 | bytes 7471104 | tf_op jit(solution)/shard_map/dot_general | solution.py:10
  169.2 0.0 copy-start.3
  169.2 4.7 %copy.18 = bf16[768,2048]{0,1:T(8,128)(2,1)} copy(bf16[768,2048]{1,0:T(8,128)(2,1)} %convolution_convert_fusion) | data formatting | bytes 6291456 | tf_op jit(solution)/shard_map/convert_element_type | solution.py:12
  173.9 0.0 copy-start.1
  173.9 0.0 copy-start.2
  173.9 3.3 %gather_fusion = bf16[128,768]{1,0:T(8,128)(2,1)S(1)} fusion(bf16[768,2048]{0,1:T(8,128)(2,1)} %copy.18, s32[1024]{0:T(1024)S(1)} %pad_clamp_fusion), kind=kCustom, calls=%fused_computation | custom fusion | bytes 393728 | tf_op jit(solution)/shard_map/jit(_take)/gather | solution.py:21
  177.2 0.2 copy.19
  177.4 0.0 copy-done.3
  177.4 0.5 fusion.10
  177.9 17.0 %all_to_all.16 = bf16[32,24,128]{2,1,0:T(8,128)(2,1)S(1)} all-to-all(bf16[32,24,128]{2,1,0:T(8,128)(2,1)S(1)} %bitcast.37), channel_id=1, replica_groups=mesh['index'=24,'ingest'=32] {'ingest'}, dimensions={0} | all-to-all | bytes 393216 | tf_op jit(solution)/shard_map/all_to_all | solution.py:24
  195.0 0.8 broadcast_in_dim.65
  195.8 0.0 all-gather.7.cloned.1.call-update
  196.5 0.0 copy-done.1
  196.5 0.1 fusion.17
  196.5 0.1 reduce_window_sum.11
  196.6 0.2 select_reduce_fusion.1
  196.8 0.0 copy-done.2
  196.8 0.1 select_reduce_fusion.2
  196.9 1.2 dynamic-slice
  198.7 0.2 dynamic-update-slice
  199.0 0.2 dynamic-update-slice.1
  199.2 88.2 %all-reduce.2 = (bf16[768]{0:T(1024)(128)(2,1)S(1)}, bf16[768]{0:T(1024)(128)(2,1)S(1)}) all-reduce(bf16[768]{0:T(1024)(128)(2,1)S(1)} %dynamic-update-slice.1, bf16[768]{0:T(1024)(128)(2,1)S(1)} %dynamic-update-slice), channel_id=3, replica_groups=mesh['index'=24,'ingest'=32] {'index'}, use_global_device_ids=true, to_apply=%add.1 | all-reduce | flops 1536 | bytes 6144
  287.4 0.1 reshape.64
  287.5 0.1 reshape.61
  287.5 20.8 %all-gather.7.cloned.1.call-done = bf16[24,24,4096]{2,1,0:T(8,128)(2,1)} async-done(((bf16[1,24,4096]{2,1,0:T(8,128)(2,1)}), bf16[24,24,4096]{2,1,0:T(8,128)(2,1)}) %all-gather.7.cloned.1.call-update) | async-done | bytes 4718608 | tf_op jit(solution)/shard_map/all_gather | solution.py:43
  308.3 3.8 %copy.23 = bf16[72,8,32,128]{3,2,1,0:T(8,128)(2,1)S(1)} copy(bf16[72,8,32,128]{3,1,2,0:T(8,128)(2,1)} %bitcast.35) | data formatting | bytes 9437184
  312.1 0.9 fusion.5
  313.0 0.2 copy.21
  313.2 1.2 reshape.49
  (10 shorter events, 0.1 us)
Async XLA Ops:
  6.5 156.7 %copy-start = (bf16[768,768]{1,0:T(8,128)(2,1)S(1)}, bf16[768,768]{1,0:T(8,128)(2,1)}, u32[]{:S(2)}) copy-start(bf16[768,768]{1,0:T(8,128)(2,1)} %param.8) | copy-start | bytes 3538948
  6.5 156.7 %all-gather.5.cloned.1.call-start = ((), (), s32[]{:S(2)}) async-start(), calls=%async_computation.1 | async-start | bytes 3244032 | tf_op jit(solution)/shard_map/all_gather | solution.py:17
  7.3 301.1 %all-gather.7.cloned.1.call-start = ((), (), s32[]{:S(2)}) async-start(), calls=%async_computation.2 | async-start | bytes 4915200 | tf_op jit(solution)/shard_map/all_gather | solution.py:43
  169.2 8.2 %copy-start.3 = (bf16[128,768]{1,0:T(8,128)(2,1)S(1)}, bf16[128,768]{1,0:T(8,128)(2,1)}, u32[]{:S(2)}) copy-start(bf16[128,768]{1,0:T(8,128)(2,1)} %param.7) | copy-start | bytes 589828
  173.9 22.5 %copy-start.1 = (s32[1,32,1]{1,2,0:T(1,128)S(1)}, s32[1,32,1]{1,2,0:T(1,128)}, u32[]{:S(2)}) copy-start(s32[1,32,1]{1,2,0:T(1,128)} %param.12) | copy-start | bytes 388
  173.9 22.8 %copy-start.2 = (s32[1,32]{1,0:T(1,128)S(1)}, s32[1,32]{1,0:T(1,128)}, u32[]{:S(2)}) copy-start(s32[1,32]{1,0:T(1,128)} %param.11) | copy-start | bytes 388
Sparse Core Ops, SparseCore 0:
  9.7 153.4 all-gather.4
  195.9 112.3 all-gather.6
where the time goes:
time: 324 us; the launch traced here: 321 us
  waiting for transfers between devices  177 us (55%)
  blocking collectives  105 us (32%)
  local copies, waits for them, and re-layouts  16 us (5%)
  between operations  14.7 us (5%)
  matrix products  7.36 us (2%)
    all_gather x1, waiting for transfers between devices, body(): piece = lax.all_gather(centroids, 'ingest', axis=0, tiled=True)  155 us
    unnamed x1, blocking collectives  88.2 us
    all_gather x1, waiting for transfers between devices, body(): slabs = lax.all_gather(grouped[None], 'index', axis=0, tiled=True)  20.8 us
    all_to_all x1, blocking collectives, body(): lax.all_to_all(residual, 'ingest', split_axis=0, concat_axis=1, tiled=True)  17 us
    dot_general x2, matrix products, turn_rows(): lax.dot_general(rotation, rows, (((0,), (1,)), ((), ())), preferred_eleme...  6.5 us
  transfers between devices with their start and end apart: 2, of which 2 were waited for; matrix products, arithmetic and copies ran while one was open for 1% of the time, Pallas kernels for 0%

commit v1 on v0

v1 whole, which is shorter than its diff:
```python
import jax
import jax.numpy as jnp
from jax import lax
from jax.experimental import pallas as pl
from jax.experimental.pallas import tpu as pltpu
from jax.sharding import PartitionSpec as P

D = 768
BROWS = 128
CAP = 3
NI = 24
NG = 32
FEAT = D // NG
HALF = 32
WIDE = CAP * BROWS
MESH = pl.DeviceIdType.MESH


def lanes(x, idx):
    return jnp.take_along_axis(x, idx, axis=1, mode="promise_in_bounds")


def kernel(vec, rot, cen, asg, order, dest, live, out,
           x, r, send, recv, tbl, grp, pos, looked, res, send2, blkv, blks,
           lsem, ssem, rsem, tsem, s2sem, r2sem):
    f32, bf16, i32 = jnp.float32, jnp.bfloat16, jnp.int32
    g = lax.axis_index("ingest")
    i = lax.axis_index("index")
    core = lax.rem(i, 2)
    zh = lax.rem(lax.div(i, 2), 3)
    xx = lax.div(i, 6)

    def peer(e):
        far = e < 16
        dz = jnp.where(far, 1 + lax.rem(e, 2), 0)
        rest = jnp.where(far, lax.div(e, 2), 23 - e)
        px = lax.rem(xx + lax.div(rest, 2), 4)
        pz = lax.rem(zh + dz, 3)
        pc = lax.rem(core + lax.rem(rest, 2), 2)
        return (px * 3 + pz) * 2 + pc

    barrier = pltpu.get_barrier_semaphore()

    @pl.loop(1, NG)
    def _(d):
        pl.semaphore_signal(barrier, inc=1, device_id={"ingest": lax.rem(g + d, NG)}, device_id_type=MESH)

    @pl.loop(0, NI - 1)
    def _(e):
        pl.semaphore_signal(barrier, inc=1, device_id={"index": peer(e)}, device_id_type=MESH)

    loads = [
        pltpu.make_async_copy(rot, r, lsem.at[0]),
        pltpu.make_async_copy(vec, x.at[pl.ds(0, BROWS)], lsem.at[1]),
    ]
    for k in range(4):
        loads.append(pltpu.make_async_copy(
            cen.at[pl.ds(pl.multiple_of(core * HALF, HALF), HALF)],
            x.at[pl.ds(BROWS + HALF * k, HALF)], lsem.at[2 + k]))
    for c in loads:
        c.start()

    sub = lax.broadcasted_iota(i32, (32, 32), 0)
    lan = lax.broadcasted_iota(i32, (32, 32), 1)
    eye = sub == lan
    d_row = jnp.broadcast_to(dest[...], (32, 32))
    d_col = jnp.sum(jnp.where(eye, d_row, 0), axis=1, keepdims=True)
    o_col = jnp.sum(jnp.where(eye, jnp.broadcast_to(order[...], (32, 32)), 0), axis=1, keepdims=True)
    n_live = live[0]
    slot = jnp.sum(jnp.where((d_row == d_col) & (lan < sub) & (lan < n_live), 1, 0), axis=1, keepdims=True)
    k_col = lax.broadcasted_iota(i32, (32, 1), 0)
    target = jnp.where(k_col < n_live, d_col * CAP + slot, -1)
    q = lax.broadcasted_iota(i32, (32, 128), 1)
    hit = target == q
    blk = jnp.sum(jnp.where(hit, o_col - NG, 0), axis=0, keepdims=True) + NG
    blkv[...] = jnp.broadcast_to(blk, (8, 128))
    to_smem = pltpu.make_async_copy(blkv, blks, lsem.at[6])
    to_smem.start()

    lane8 = lax.broadcasted_iota(i32, (8, 128), 1)
    sub8 = lax.broadcasted_iota(i32, (8, 128), 0)
    slot8 = lax.div(lane8, 32)
    low8 = lax.rem(lane8, 32)

    a = lanes(jnp.broadcast_to(asg[...], (8, 128)), lax.rem(sub8, 4) * 32 + low8)
    a_grp = (lax.shift_right_logical(a, 5) & 1) * 8 + lax.shift_right_logical(a, 8)
    a_pos = (lax.shift_right_logical(a, 6) & 3) * 32 + (a & 31)
    a_val = jnp.where(sub8 < 4, a_grp, a_pos).astype(f32)

    for c in loads:
        c.wait()
    y = jnp.dot(x[...], r[...], preferred_element_type=f32).astype(bf16).astype(f32)
    yt = y.T
    rt = yt[:, :BROWS].reshape(NG, FEAT, BROWS)
    tt = yt[:, BROWS:].reshape(NG, FEAT, BROWS)
    turn = lax.rem(slot8 + 4 - lax.rem(g, 4), 4)[None]
    tail = jnp.where(turn == 0, tt[:, 0:8], jnp.where(turn == 1, tt[:, 8:16], jnp.where(turn == 2, tt[:, 16:24], a_val[None])))
    send[...] = jnp.concatenate([rt, tail], axis=1).astype(bf16)

    pl.semaphore_wait(barrier, NG + NI - 2)

    @pl.loop(1, NG)
    def _(d):
        to = lax.rem(g + d, NG)
        pltpu.make_async_remote_copy(
            src_ref=send.at[to], dst_ref=recv.at[g], send_sem=ssem, recv_sem=rsem,
            device_id={"ingest": to}, device_id_type=MESH).start()

    recv[pl.ds(g, 1)] = send[pl.ds(g, 1)]
    res[NG] = jnp.zeros((FEAT, BROWS), bf16)
    to_smem.wait()

    some = pltpu.make_async_remote_copy(
        src_ref=send.at[pl.ds(0, NG - 1)], dst_ref=recv.at[pl.ds(0, NG - 1)], send_sem=ssem, recv_sem=rsem,
        device_id={"ingest": lax.rem(g + 1, NG)}, device_id_type=MESH)
    some.wait_recv()

    @pl.loop(0, NG // 4)
    def _(quad):
        m = [recv[quad * 4 + j].astype(f32)[24:32] for j in range(4)]
        turned = []
        for f in range(4):
            t = m[3]
            for j in range(3):
                t = jnp.where(slot8 == (f + j) % 4, m[j], t)
            turned.append(t)
        tbl[core, quad] = jnp.concatenate(turned[:3], axis=0).astype(bf16)
        for j in range(4):
            v = lanes(turned[3], 32 * ((3 + j) % 4) + low8)
            grp[pl.ds(quad * 4 + j, 1)] = jnp.sum(jnp.where(sub8 == slot8, v, 0.0), axis=0, keepdims=True).astype(i32)
            pos[pl.ds(quad * 4 + j, 1)] = jnp.sum(jnp.where(sub8 == slot8 + 4, v, 0.0), axis=0, keepdims=True).astype(i32)

    other = lax.rem(core + 1, 2)
    swap = pltpu.make_async_remote_copy(
        src_ref=tbl.at[core], dst_ref=tbl.at[core], send_sem=tsem.at[0], recv_sem=tsem.at[1],
        device_id={"index": i + 1 - 2 * core}, device_id_type=MESH)
    swap.start()

    def look(half, first):
        table = [tbl[half, quad].astype(f32) for quad in range(NG // 4)]

        @pl.loop(0, NG)
        def _(b):
            lane0 = jnp.broadcast_to(pos[pl.ds(b, 1)], (8, 128))
            want = jnp.broadcast_to(grp[pl.ds(b, 1)], (8, 128)) - half * (NG // 4)
            outs = []
            for f in range(3):
                idx = (lane0 + 32 * f) & 127
                acc = jnp.zeros((8, 128), f32) if first else looked[b, 8 * f:8 * f + 8]
                for quad in range(NG // 4):
                    acc = jnp.where(want == quad, lanes(table[quad][8 * f:8 * f + 8], idx), acc)
                outs.append(acc)
            got = jnp.concatenate(outs, axis=0)
            if first:
                looked[b] = got
            else:
                res[b] = (recv[b].astype(f32)[:FEAT] - got).astype(bf16)

    look(core, True)
    pltpu.make_async_remote_copy(
        src_ref=tbl.at[other], dst_ref=tbl.at[other], send_sem=tsem.at[0], recv_sem=tsem.at[1],
        device_id={"index": i + 1 - 2 * core}, device_id_type=MESH).wait_recv()
    look(other, False)

    def pack(p):
        for s in range(CAP):
            send2[p, :, s * BROWS:(s + 1) * BROWS] = res[blks[0, p * CAP + s]]

    columns = pl.ds(pl.multiple_of(i * WIDE, WIDE), WIDE)

    @pl.loop(0, NI - 1)
    def _(e):
        p = peer(e)
        pack(p)
        pltpu.make_async_remote_copy(
            src_ref=send2.at[p], dst_ref=out.at[:, columns], send_sem=s2sem.at[e], recv_sem=r2sem.at[e],
            device_id={"index": p}, device_id_type=MESH).start()

    pack(i)
    own = pltpu.make_async_copy(send2.at[i], out.at[:, columns], lsem.at[7])
    own.start()
    some.wait_send()
    swap.wait_send()
    own.wait()

    @pl.loop(0, NI - 1)
    def _(e):
        c = pltpu.make_async_remote_copy(
            src_ref=send2.at[0], dst_ref=out.at[:, pl.ds(0, WIDE)], send_sem=s2sem.at[e], recv_sem=r2sem.at[e],
            device_id={"index": peer(e)}, device_id_type=MESH)
        c.wait_send()
        c.wait_recv()


def body(vectors, rotation, centroids, assignment, block_order, destination, live_count):
    bf16, f32, i32 = jnp.bfloat16, jnp.float32, jnp.int32
    anywhere = pl.BlockSpec(memory_space=pl.ANY)
    vmem = pl.BlockSpec(memory_space=pltpu.VMEM)
    smem = pl.BlockSpec(memory_space=pltpu.SMEM)
    dma = pltpu.SemaphoreType.DMA
    return pl.pallas_call(
        kernel,
        out_shape=jax.ShapeDtypeStruct((FEAT, NI * WIDE), bf16),
        in_specs=[anywhere, anywhere, anywhere, vmem, vmem, vmem, smem],
        out_specs=anywhere,
        scratch_shapes=[
            pltpu.VMEM((2 * BROWS, D), bf16),
            pltpu.VMEM((D, D), bf16),
            pltpu.VMEM((NG, 32, BROWS), bf16),
            pltpu.VMEM((NG, 32, BROWS), bf16),
            pltpu.VMEM((2, NG // 4, FEAT, 128), bf16),
            pltpu.VMEM((NG, 128), i32),
            pltpu.VMEM((NG, 128), i32),
            pltpu.VMEM((NG, FEAT, 128), f32),
            pltpu.VMEM((NG + 1, FEAT, BROWS), bf16),
            pltpu.VMEM((NI, FEAT, WIDE), bf16),
            pltpu.VMEM((8, 128), i32),
            pltpu.SMEM((8, 128), i32),
            dma((8,)), dma, dma, dma((2,)), dma((NI,)), dma((NI,)),
        ],
        compiler_params=pltpu.CompilerParams(
            collective_id=0, has_side_effects=True, vmem_limit_bytes=32 * 1024 * 1024),
        name="route",
    )(vectors, rotation, centroids, assignment.reshape(1, BROWS), block_order, destination.reshape(1, 32), live_count)


def solution(mesh):
    return jax.shard_map(
        body,
        mesh=mesh,
        in_specs=(
            P(("index", "ingest"), None),
            P(),
            P("ingest", None),
            P(("index", "ingest")),
            P("index", None),
            P("index", None, None),
            P("index"),
        ),
        out_specs=P("ingest", "index"),
        check_vma=False,
    )
```

time: 324 us -> 58.1 us (0.18)
  waiting for transfers between devices: 177 us -> 0 us
  blocking collectives: 105 us -> 0 us
  Pallas kernels: 0 us -> 51.2 us
  between operations: 14.7 us -> 0.67 us
  local copies, waits for them, and re-layouts: 16 us -> 5.81 us
  matrix products: 7.36 us -> 0 us
    all_gather x2 -> x0, waiting for transfers between devices: 176 us -> none  [the longest x1 155 us: body(): piece = lax.all_gather(centroids, 'ingest', axis=0, tiled=True)]
    unnamed x1 -> x0, blocking collectives: 88.2 us -> none
    pallas_call x0 -> x1, Pallas kernels: none -> 51.2 us  [body(): pl.pallas_call(kernel, out_shape=jax.ShapeDtypeStruct((FEAT, NI * WIDE),...]
    all_to_all x1 -> x0, blocking collectives: 17 us -> none  [body(): lax.all_to_all(residual, 'ingest', split_axis=0, concat_axis=1, tiled=True)]
    dot_general x3 -> x0, matrix products: 7.36 us -> none  [the longest x2 6.5 us: turn_rows(): lax.dot_general(rotation, rows, (((0,), (1,)), ((), ())), preferred_eleme...]
    convert_element_type x3 -> x0, local copies, waits for them, and re-layouts: 5.01 us -> none  [the longest x1 4.73 us: turn_rows(): return lax.dot_general(rotation, rows, (((0,), (1,)), ((), ())), preferre...]
    gather x2 -> x0, local copies, waits for them, and re-layouts: 3.45 us -> none  [body(): taken = jnp.take(turned, jnp.clip(assignment, 0, width - 1), axis=1)]
  transfers between devices with their start and end apart: 2 -> 0, of which waited for: 2 -> 0; matrix products, arithmetic and copies ran while one was open for 1% -> 0% of each run, Pallas kernels for 0% -> 0%
where the time goes in v1:
time: 58.1 us; the launch traced here: 57.7 us
  Pallas kernels  51.2 us (88%)
  local copies, waits for them, and re-layouts  5.81 us (10%)
  between operations  0.67 us (1%)
    pallas_call x1, Pallas kernels, body(): pl.pallas_call(kernel, out_shape=jax.ShapeDtypeStruct((FEAT, NI * WIDE),...  51.2 us
    unnamed x13, local copies, waits for them, and re-layouts  5.81 us

profile of v1, /device:TPU:1, one launch (start us, length us, event | category | flops | bytes accessed | tf_op | source)
XLA Modules:
  0.0 57.7 jit_solution(1030091416128545385)
XLA Ops:
  0.7 0.0 copy-start
  0.7 1.3 %copy-done = bf16[768,768]{1,0:T(8,128)(2,1)S(1)} copy-done((bf16[768,768]{1,0:T(8,128)(2,1)S(1)}, bf16[768,768]{1,0:T(8,128)(2,1)}, u32[]{:S(2)}) %copy-start) | copy-done | bytes 1179672
  1.9 0.0 copy-start.1
  1.9 0.9 %copy-done.1 = bf16[128,768]{1,0:T(8,128)(2,1)S(1)} copy-done((bf16[128,768]{1,0:T(8,128)(2,1)S(1)}, bf16[128,768]{1,0:T(8,128)(2,1)}, u32[]{:S(2)}) %copy-start.1) | copy-done | bytes 196632
  2.9 0.0 copy-start.2
  2.9 0.9 %copy-done.2 = bf16[64,768]{1,0:T(8,128)(2,1)S(1)} copy-done((bf16[64,768]{1,0:T(8,128)(2,1)S(1)}, bf16[64,768]{1,0:T(8,128)(2,1)}, u32[]{:S(2)}) %copy-start.2) | copy-done | bytes 98328
  3.7 0.0 copy-start.3
  3.7 0.7 %copy-done.3 = s32[128]{0:T(128)S(1)} copy-done((s32[128]{0:T(128)S(1)}, s32[128]{0:T(128)}, u32[]{:S(2)}) %copy-start.3) | copy-done | bytes 536
  4.4 0.0 copy-start.4
  4.4 0.7 %copy-done.4 = s32[1,32]{1,0:T(1,128)S(1)} copy-done((s32[1,32]{1,0:T(1,128)S(1)}, s32[1,32]{1,0:T(1,128)}, u32[]{:S(2)}) %copy-start.4) | copy-done | bytes 152
  5.1 0.0 copy-start.5
  5.1 0.7 %copy-done.5 = s32[1,32,1]{1,2,0:T(1,128)S(1)} copy-done((s32[1,32,1]{1,2,0:T(1,128)S(1)}, s32[1,32,1]{1,2,0:T(1,128)}, u32[]{:S(2)}) %copy-start.5) | copy-done | bytes 152
  5.7 51.2 %route.1 = bf16[24,9216]{1,0:T(8,128)(2,1)S(1)} custom-call(bf16[128,768]{1,0:T(8,128)(2,1)S(1)} %copy-done.1, bf16[768,768]{1,0:T(8,128)(2,1)S(1)} %copy-done, bf16[64,768]{1,0:T(8,128)(2,1)S(1)} %copy-done.2, s32[1,128]{1,0:T(1,128)S(1)} %bitcast.2, s32[1,32]{1,0:T(1,128)S(1)} %copy-done.4, s32[1,32]{1,0:T(1,128)S(1)} %bitcast.3, s32[1]{0:T(128)S(6)} %copy.9.live), custom_call_target="tpu_custom_call" | custom-call | tf_op jit(solution)/shard_map/route/pallas_call | solution.py:201
  56.9 0.8 %copy.10 = bf16[24,9216]{1,0:T(8,128)(2,1)} copy(bf16[24,9216]{1,0:T(8,128)(2,1)S(1)} %route.1) | data formatting | bytes 884736
Async XLA Ops:
  0.7 1.3 %copy-start = (bf16[768,768]{1,0:T(8,128)(2,1)S(1)}, bf16[768,768]{1,0:T(8,128)(2,1)}, u32[]{:S(2)}) copy-start(bf16[768,768]{1,0:T(8,128)(2,1)} %rot.1) | copy-start | bytes 3538948
  1.9 0.9 %copy-start.1 = (bf16[128,768]{1,0:T(8,128)(2,1)S(1)}, bf16[128,768]{1,0:T(8,128)(2,1)}, u32[]{:S(2)}) copy-start(bf16[128,768]{1,0:T(8,128)(2,1)} %vec.1) | copy-start | bytes 589828
  2.9 0.9 %copy-start.2 = (bf16[64,768]{1,0:T(8,128)(2,1)S(1)}, bf16[64,768]{1,0:T(8,128)(2,1)}, u32[]{:S(2)}) copy-start(bf16[64,768]{1,0:T(8,128)(2,1)} %cen.1) | copy-start | bytes 294916
  3.7 0.7 %copy-start.3 = (s32[128]{0:T(128)S(1)}, s32[128]{0:T(128)}, u32[]{:S(2)}) copy-start(s32[128]{0:T(128)} %param.10) | copy-start | bytes 1540
  4.4 0.7 %copy-start.4 = (s32[1,32]{1,0:T(1,128)S(1)}, s32[1,32]{1,0:T(1,128)}, u32[]{:S(2)}) copy-start(s32[1,32]{1,0:T(1,128)} %order.1) | copy-start | bytes 388
  5.1 0.7 %copy-start.5 = (s32[1,32,1]{1,2,0:T(1,128)S(1)}, s32[1,32,1]{1,2,0:T(1,128)}, u32[]{:S(2)}) copy-start(s32[1,32,1]{1,2,0:T(1,128)} %param.12) | copy-start | bytes 388

commit v2 on v1

v2 whole, which is shorter than its diff:
```python
import jax
import jax.numpy as jnp
from jax import lax
from jax.experimental import pallas as pl
from jax.experimental.pallas import tpu as pltpu
from jax.sharding import PartitionSpec as P

D = 768
BROWS = 128
CAP = 3
NI = 24
NG = 32
FEAT = D // NG
OCT = FEAT // 8
QUADS = NG // 4
FIRST = 2
HALF = 32
WIDE = CAP * BROWS
MESH = pl.DeviceIdType.MESH


def lanes(x, idx):
    return jnp.take_along_axis(x, idx, axis=1, mode="promise_in_bounds")


def kernel(vec, rot, cen, asg_in, order_in, dest_in, live, out,
           asg, order, dest, x, r, send, recv, sent_tail, tail_in, tbl, grp, pos, looked, send2, blkv, blks,
           lsem, s1, r1, swap_sem, s2, r2, entered, paired):
    f32, bf16, i32 = jnp.float32, jnp.bfloat16, jnp.int32
    g = lax.axis_index("ingest")
    i = lax.axis_index("index")
    core = i & 1
    chip = lax.shift_right_logical(i, 1)
    xx = lax.div(chip, 3)
    zh = chip - 3 * xx
    other = 1 - core
    spot = xx * 2 + core
    rank = zh * 8 + spot

    def ingest_peer(t):
        n = t >> 2
        dy = jnp.where((n & 1) == 0, 4 + (n >> 1), 3 - (n >> 1))
        return (((g >> 2) + dy) & 7) * 4 + ((g & 3) ^ (3 - (t & 3)))

    def owner(z, x_, c):
        return (x_ * 3 + z) * 2 + c

    sibling = owner(zh, xx, other)
    small = [
        pltpu.make_async_copy(a, b, lsem.at[8 + k])
        for k, (a, b) in enumerate(((asg_in, asg), (order_in, order), (dest_in, dest)))]
    for c in small:
        c.start()
    loads = [
        pltpu.make_async_copy(rot, r, lsem.at[0]),
        pltpu.make_async_copy(vec, x.at[pl.ds(0, BROWS)], lsem.at[1]),
    ]
    for k in range(4):
        loads.append(pltpu.make_async_copy(
            cen.at[pl.ds(pl.multiple_of(core * HALF, HALF), HALF)],
            x.at[pl.ds(BROWS + HALF * k, HALF)], lsem.at[2 + k]))
    for c in loads:
        c.start()

    barrier = pltpu.get_barrier_semaphore()

    @pl.loop(0, NG - 1, unroll=31)
    def _(t):
        pl.semaphore_signal(barrier, inc=1, device_id={"ingest": ingest_peer(t)}, device_id_type=MESH)

    @pl.loop(rank + 1, NI)
    def _(n):
        pl.semaphore_signal(
            barrier, inc=1, device_id={"index": owner(n >> 3, (n >> 1) & 3, n & 1)}, device_id_type=MESH)

    for c in small:
        c.wait()
    sub = lax.broadcasted_iota(i32, (32, 32), 0)
    lan = lax.broadcasted_iota(i32, (32, 32), 1)
    eye = sub == lan
    d_row = jnp.broadcast_to(dest[...], (32, 32))
    d_col = jnp.sum(jnp.where(eye, d_row, 0), axis=1, keepdims=True)
    o_col = jnp.sum(jnp.where(eye, jnp.broadcast_to(order[...], (32, 32)), 0), axis=1, keepdims=True)
    n_live = live[0]
    slot = jnp.sum(jnp.where((d_row == d_col) & (lan < sub) & (lan < n_live), 1, 0), axis=1, keepdims=True)
    k_col = lax.broadcasted_iota(i32, (32, 1), 0)
    target = jnp.where(k_col < n_live, d_col * CAP + slot, -1)
    q = lax.broadcasted_iota(i32, (32, 128), 1)
    blk = jnp.sum(jnp.where(target == q, o_col - NG, 0), axis=0, keepdims=True) + NG
    blkv[...] = jnp.broadcast_to(blk, (8, 128))
    to_smem = pltpu.make_async_copy(blkv, blks, lsem.at[6])
    to_smem.start()

    lane8 = lax.broadcasted_iota(i32, (8, 128), 1)
    sub8 = lax.broadcasted_iota(i32, (8, 128), 0)
    slot8 = lane8 >> 5
    low8 = lane8 & 31

    a = lanes(jnp.broadcast_to(asg[...], (8, 128)), (sub8 & 3) * 32 + low8)
    a_grp = ((a >> 5) & 1) * QUADS + (a >> 8)
    a_pos = ((a >> 6) & 3) * 32 + (a & 31)
    a_val = jnp.where(sub8 < 4, a_grp, a_pos).astype(f32)

    for c in loads:
        c.wait()
    y = jnp.dot(x[...], r[...], preferred_element_type=f32).astype(bf16).astype(f32)
    yt = y.T
    rt = yt[:, :BROWS].reshape(NG, OCT, 8, BROWS)
    tt = yt[:, BROWS:].reshape(NG, OCT, 8, BROWS)
    turn = ((slot8 - g) & 3)[None]
    tail = jnp.where(turn == 0, tt[:, 0], jnp.where(turn == 1, tt[:, 1], jnp.where(turn == 2, tt[:, 2], a_val[None])))
    sent_tail[...] = tail.astype(bf16)
    send[...] = rt.astype(bf16)

    pl.semaphore_wait(barrier, NG - 1 + rank)

    def scatter(k, src, dst):
        @pl.loop(0, NG - 1, unroll=31)
        def _(t):
            to = ingest_peer(t)
            pltpu.make_async_remote_copy(
                src_ref=src.at[to], dst_ref=dst.at[g], send_sem=s1.at[k], recv_sem=r1.at[k],
                device_id={"ingest": to}, device_id_type=MESH).start()

        return pltpu.make_async_remote_copy(
            src_ref=src.at[pl.ds(0, NG - 1)], dst_ref=dst.at[pl.ds(0, NG - 1)],
            send_sem=s1.at[k], recv_sem=r1.at[k],
            device_id={"ingest": (g + 1) & (NG - 1)}, device_id_type=MESH)

    tails = scatter(0, sent_tail, tail_in)
    features = scatter(1, send, recv)

    @pl.when(core == 1)
    def _():
        pl.semaphore_signal(paired, inc=1, device_id={"index": sibling}, device_id_type=MESH)

    @pl.loop(0, rank)
    def _(n):
        pl.semaphore_signal(
            entered.at[zh], inc=1, device_id={"index": owner(n >> 3, (n >> 1) & 3, n & 1)}, device_id_type=MESH)

    tail_in[pl.ds(g, 1)] = sent_tail[pl.ds(g, 1)]
    recv[pl.ds(g, 1)] = send[pl.ds(g, 1)]
    recv[NG] = jnp.zeros((OCT, 8, BROWS), bf16)
    looked[NG] = jnp.zeros((OCT, 8, BROWS), f32)
    to_smem.wait()

    tails.wait_recv()
    for quad in range(QUADS):
        m = [tail_in[quad * 4 + j].astype(f32) for j in range(4)]
        for f in range(4):
            t = m[3]
            for j in range(3):
                t = jnp.where(slot8 == (f + j) % 4, m[j], t)
            if f < OCT:
                tbl[core, quad, f] = t.astype(bf16)
        for j in range(4):
            v = lanes(t, 32 * ((3 + j) % 4) + low8)
            b = quad * 4 + j
            grp[b:b + 1] = jnp.sum(jnp.where(sub8 == slot8, v, 0.0), axis=0, keepdims=True).astype(i32)
            pos[b:b + 1] = jnp.sum(jnp.where(sub8 == slot8 + 4, v, 0.0), axis=0, keepdims=True).astype(i32)

    def swap(half):
        return pltpu.make_async_remote_copy(
            src_ref=tbl.at[half], dst_ref=tbl.at[half], send_sem=swap_sem.at[0], recv_sem=swap_sem.at[1],
            device_id={"index": sibling}, device_id_type=MESH)

    @pl.when(core == 0)
    def _():
        pl.semaphore_wait(paired, 1)

    swap(core).start()

    def look(half, first):
        table = [[tbl[half, quad, f].astype(f32) for f in range(OCT)] for quad in range(QUADS)]

        @pl.loop(0, NG, unroll=8)
        def _(b):
            lane0 = jnp.broadcast_to(pos[pl.ds(b, 1)], (8, 128))
            want = jnp.broadcast_to(grp[pl.ds(b, 1)], (8, 128)) - half * QUADS
            for f in range(OCT):
                idx = (lane0 + 32 * f) & 127
                acc = jnp.zeros((8, 128), f32) if first else looked[b, f]
                for quad in range(QUADS):
                    acc = jnp.where(want == quad, lanes(table[quad][f], idx), acc)
                looked[b, f] = acc

    look(core, True)
    swap(other).wait_recv()
    look(other, False)

    columns = pl.ds(pl.multiple_of(i * WIDE, WIDE), WIDE)

    def pack(p):
        for f in range(OCT):
            for s in range(CAP):
                b = blks[0, p * CAP + s]
                send2[p, f, :, s * BROWS:(s + 1) * BROWS] = (recv[b, f].astype(f32) - looked[b, f]).astype(bf16)

    def deliver(z, x_, c, sent):
        p = owner(z, x_, c)
        pack(p)
        pltpu.make_async_remote_copy(
            src_ref=send2.at[p], dst_ref=out.at[:, :, columns], send_sem=s2.at[sent], recv_sem=r2,
            device_id={"index": p}, device_id_type=MESH).start()

    features.wait_recv()

    def messages(n, sent):
        some = out.at[:, :, pl.ds(0, n * WIDE)]
        return pltpu.make_async_remote_copy(
            src_ref=some, dst_ref=some, send_sem=s2.at[sent], recv_sem=r2,
            device_id={"index": sibling}, device_id_type=MESH)

    def far(z, sent):
        @pl.when(z > zh)
        def _():
            pl.semaphore_wait(entered.at[z], 8)

        @pl.loop(0, 8)
        def _(m):
            deliver(z, (xx + ((m >> 1) ^ 2)) & 3, core ^ (m & 1), sent)

    step = 1 + jnp.where((g & 3) < FIRST, 1, 0)
    z0 = zh + step
    z0 = jnp.where(z0 >= 3, z0 - 3, z0)
    far(z0, 0)

    @pl.when(spot < 7)
    def _():
        pl.semaphore_wait(entered.at[zh], 7 - spot)

    @pl.loop(1, 8)
    def _(m):
        deliver(zh, (xx + (m >> 1)) & 3, core ^ (m & 1), 1)

    far(3 - zh - z0, 1)

    pack(i)
    own = pltpu.make_async_copy(send2.at[i], out.at[:, :, columns], lsem.at[7])
    own.start()
    tails.wait_send()
    features.wait_send()
    swap(core).wait_send()
    own.wait()

    messages(8, 0).wait_send()
    messages(NI - 9, 1).wait_send()
    messages(NI - 1, 1).wait_recv()


def body(vectors, rotation, centroids, assignment, block_order, destination, live_count):
    bf16, f32, i32 = jnp.bfloat16, jnp.float32, jnp.int32
    hbm = pl.BlockSpec(memory_space=pltpu.HBM)
    smem = pl.BlockSpec(memory_space=pltpu.SMEM)
    dma = pltpu.SemaphoreType.DMA
    arrays = [
        pltpu.with_memory_space_constraint(a, pltpu.HBM)
        for a in (vectors, rotation, centroids, assignment.reshape(1, BROWS), block_order, destination.reshape(1, NG))]
    rebalanced = pl.pallas_call(
        kernel,
        out_shape=jax.ShapeDtypeStruct((OCT, 8, NI * WIDE), bf16),
        in_specs=[hbm] * 6 + [smem],
        out_specs=pl.BlockSpec(memory_space=pl.ANY),
        scratch_shapes=[
            pltpu.VMEM((1, BROWS), i32),
            pltpu.VMEM((1, NG), i32),
            pltpu.VMEM((1, NG), i32),
            pltpu.VMEM((2 * BROWS, D), bf16),
            pltpu.VMEM((D, D), bf16),
            pltpu.VMEM((NG, OCT, 8, BROWS), bf16),
            pltpu.VMEM((NG + 1, OCT, 8, BROWS), bf16),
            pltpu.VMEM((NG, 8, BROWS), bf16),
            pltpu.VMEM((NG, 8, BROWS), bf16),
            pltpu.VMEM((2, QUADS, OCT, 8, 128), bf16),
            pltpu.VMEM((NG, 128), i32),
            pltpu.VMEM((NG, 128), i32),
            pltpu.VMEM((NG + 1, OCT, 8, 128), f32),
            pltpu.VMEM((NI, OCT, 8, WIDE), bf16),
            pltpu.VMEM((8, 128), i32),
            pltpu.SMEM((8, 128), i32),
            dma((11,)), dma((2,)), dma((2,)), dma((2,)), dma((2,)), dma,
            pltpu.SemaphoreType.REGULAR((3,)), pltpu.SemaphoreType.REGULAR,
        ],
        compiler_params=pltpu.CompilerParams(
            collective_id=0, has_side_effects=True, vmem_limit_bytes=40 * 1024 * 1024),
        name="route",
    )(*arrays, live_count)
    return rebalanced.reshape(FEAT, NI * WIDE)


def solution(mesh):
    return jax.shard_map(
        body,
        mesh=mesh,
        in_specs=(
            P(("index", "ingest"), None),
            P(),
            P("ingest", None),
            P(("index", "ingest")),
            P("index", None),
            P("index", None, None),
            P("index"),
        ),
        out_specs=P("ingest", "index"),
        check_vma=False,
    )
```

time: 58.1 us -> 47.4 us (0.82)
  Pallas kernels: 51.2 us -> 45.8 us
  local copies, waits for them, and re-layouts: 5.81 us -> 0.76 us
    pallas_call x1, Pallas kernels: 51.2 us -> 45.8 us  [body(): pl.pallas_call(kernel, out_shape=jax.ShapeDtypeStruct((OCT, 8, NI * WIDE)...]
    unnamed x13 -> x1, local copies, waits for them, and re-layouts: 5.81 us -> 0.76 us
where the time goes in v2:
time: 47.4 us; the launch traced here: 47.2 us
  Pallas kernels  45.8 us (97%)
  local copies, waits for them, and re-layouts  0.76 us (2%)
  between operations  0.66 us (1%)
    pallas_call x1, Pallas kernels, body(): pl.pallas_call(kernel, out_shape=jax.ShapeDtypeStruct((OCT, 8, NI * WIDE)...  45.8 us

profile of v2, /device:TPU:1, one launch (start us, length us, event | category | flops | bytes accessed | tf_op | source)
XLA Modules:
  0.0 47.2 jit_solution(7848091238882821593)
XLA Ops:
  0.7 45.8 %route.1 = bf16[3,8,9216]{2,1,0:T(8,128)(2,1)S(1)} custom-call(bf16[128,768]{1,0:T(8,128)(2,1)} %vec.1, bf16[768,768]{1,0:T(8,128)(2,1)} %rot.1, bf16[64,768]{1,0:T(8,128)(2,1)} %cen.1, s32[1,128]{1,0:T(1,128)} %bitcast.4, s32[1,32]{1,0:T(1,128)} %order_in.1, s32[1,32]{1,0:T(1,128)} %bitcast.5, s32[1]{0:T(128)S(6)} %copy.9.live), custom_call_target="tpu_custom_call" | custom-call | tf_op jit(solution)/shard_map/route/pallas_call | solution.py:260
  46.5 0.8 %copy.10 = bf16[24,9216]{1,0:T(8,128)(2,1)} copy(bf16[24,9216]{1,0:T(8,128)(2,1)S(1)} %bitcast.3) | data formatting | bytes 884736

commit v3 on v2

--- a/solution.py
+++ b/solution.py
@@ -14,6 +14,7 @@
 OCT = FEAT // 8
 QUADS = NG // 4
 FIRST = 2
+AHEAD = 1
 HALF = 32
 WIDE = CAP * BROWS
 MESH = pl.DeviceIdType.MESH
@@ -46,6 +47,12 @@
         return (x_ * 3 + z) * 2 + c
 
     sibling = owner(zh, xx, other)
+    barrier = pltpu.get_barrier_semaphore()
+
+    @pl.loop(0, NG - 1, unroll=31)
+    def _(t):
+        pl.semaphore_signal(barrier, inc=1, device_id={"ingest": ingest_peer(t)}, device_id_type=MESH)
+
     small = [
         pltpu.make_async_copy(a, b, lsem.at[8 + k])
         for k, (a, b) in enumerate(((asg_in, asg), (order_in, order), (dest_in, dest)))]
@@ -61,12 +68,6 @@
             x.at[pl.ds(BROWS + HALF * k, HALF)], lsem.at[2 + k]))
     for c in loads:
         c.start()
-
-    barrier = pltpu.get_barrier_semaphore()
-
-    @pl.loop(0, NG - 1, unroll=31)
-    def _(t):
-        pl.semaphore_signal(barrier, inc=1, device_id={"ingest": ingest_peer(t)}, device_id_type=MESH)
 
     @pl.loop(rank + 1, NI)
     def _(n):
@@ -127,9 +128,6 @@
             send_sem=s1.at[k], recv_sem=r1.at[k],
             device_id={"ingest": (g + 1) & (NG - 1)}, device_id_type=MESH)
 
-    tails = scatter(0, sent_tail, tail_in)
-    features = scatter(1, send, recv)
-
     @pl.when(core == 1)
     def _():
         pl.semaphore_signal(paired, inc=1, device_id={"index": sibling}, device_id_type=MESH)
@@ -138,6 +136,10 @@
     def _(n):
         pl.semaphore_signal(
             entered.at[zh], inc=1, device_id={"index": owner(n >> 3, (n >> 1) & 3, n & 1)}, device_id_type=MESH)
+
+    tails = scatter(0, sent_tail, tail_in)
+    features = scatter(1, send, recv)
+
 
     tail_in[pl.ds(g, 1)] = sent_tail[pl.ds(g, 1)]
     recv[pl.ds(g, 1)] = send[pl.ds(g, 1)]
@@ -146,6 +148,7 @@
     to_smem.wait()
 
     tails.wait_recv()
+    slips = []
     for quad in range(QUADS):
         m = [tail_in[quad * 4 + j].astype(f32) for j in range(4)]
         for f in range(4):
@@ -154,11 +157,7 @@
                 t = jnp.where(slot8 == (f + j) % 4, m[j], t)
             if f < OCT:
                 tbl[core, quad, f] = t.astype(bf16)
-        for j in range(4):
-            v = lanes(t, 32 * ((3 + j) % 4) + low8)
-            b = quad * 4 + j
-            grp[b:b + 1] = jnp.sum(jnp.where(sub8 == slot8, v, 0.0), axis=0, keepdims=True).astype(i32)
-            pos[b:b + 1] = jnp.sum(jnp.where(sub8 == slot8 + 4, v, 0.0), axis=0, keepdims=True).astype(i32)
+        slips.append(t)
 
     def swap(half):
         return pltpu.make_async_remote_copy(
@@ -171,10 +170,15 @@
 
     swap(core).start()
 
+    for b in range(NG):
+        v = lanes(slips[b // 4], 32 * ((3 + b) % 4) + low8)
+        grp[b:b + 1] = jnp.sum(jnp.where(sub8 == slot8, v, 0.0), axis=0, keepdims=True).astype(i32)
+        pos[b:b + 1] = jnp.sum(jnp.where(sub8 == slot8 + 4, v, 0.0), axis=0, keepdims=True).astype(i32)
+
     def look(half, first):
         table = [[tbl[half, quad, f].astype(f32) for f in range(OCT)] for quad in range(QUADS)]
 
-        @pl.loop(0, NG, unroll=8)
+        @pl.loop(0, NG, unroll=16)
         def _(b):
             lane0 = jnp.broadcast_to(pos[pl.ds(b, 1)], (8, 128))
             want = jnp.broadcast_to(grp[pl.ds(b, 1)], (8, 128)) - half * QUADS
@@ -212,19 +216,21 @@
             src_ref=some, dst_ref=some, send_sem=s2.at[sent], recv_sem=r2,
             device_id={"index": sibling}, device_id_type=MESH)
 
-    def far(z, sent):
+    def far(z, ahead):
         @pl.when(z > zh)
         def _():
             pl.semaphore_wait(entered.at[z], 8)
 
         @pl.loop(0, 8)
         def _(m):
-            deliver(z, (xx + ((m >> 1) ^ 2)) & 3, core ^ (m & 1), sent)
+            k = m >> 1
+            x_ = (xx + jnp.where(k < 2, k + 2, 3 - k)) & 3
+            deliver(z, x_, core ^ (m & 1), jnp.where(m < ahead, 0, 1))
 
     step = 1 + jnp.where((g & 3) < FIRST, 1, 0)
     z0 = zh + step
     z0 = jnp.where(z0 >= 3, z0 - 3, z0)
-    far(z0, 0)
+    far(z0, AHEAD)
 
     @pl.when(spot < 7)
     def _():
@@ -234,7 +240,7 @@
     def _(m):
         deliver(zh, (xx + (m >> 1)) & 3, core ^ (m & 1), 1)
 
-    far(3 - zh - z0, 1)
+    far(3 - zh - z0, 0)
 
     pack(i)
     own = pltpu.make_async_copy(send2.at[i], out.at[:, :, columns], lsem.at[7])
@@ -244,8 +250,8 @@
     swap(core).wait_send()
     own.wait()
 
-    messages(8, 0).wait_send()
-    messages(NI - 9, 1).wait_send()
+    messages(AHEAD, 0).wait_send()
+    messages(NI - 1 - AHEAD, 1).wait_send()
     messages(NI - 1, 1).wait_recv()
 
 

time: 47.4 us -> 45.1 us (0.951)
  Pallas kernels: 45.8 us -> 43.5 us
    pallas_call x1, Pallas kernels: 45.8 us -> 43.5 us  [body(): pl.pallas_call(kernel, out_shape=jax.ShapeDtypeStruct((OCT, 8, NI * WIDE)...]
where the time goes in v3:
time: 45.1 us; the launch traced here: 44.9 us
  Pallas kernels  43.5 us (96%)
  local copies, waits for them, and re-layouts  0.76 us (2%)
  between operations  0.66 us (1%)
    pallas_call x1, Pallas kernels, body(): pl.pallas_call(kernel, out_shape=jax.ShapeDtypeStruct((OCT, 8, NI * WIDE)...  43.5 us

profile of v3, /device:TPU:1, one launch (start us, length us, event | category | flops | bytes accessed | tf_op | source)
XLA Modules:
  0.0 44.9 jit_solution(3589108491697441533)
XLA Ops:
  0.7 43.5 %route.1 = bf16[3,8,9216]{2,1,0:T(8,128)(2,1)S(1)} custom-call(bf16[128,768]{1,0:T(8,128)(2,1)} %vec.1, bf16[768,768]{1,0:T(8,128)(2,1)} %rot.1, bf16[64,768]{1,0:T(8,128)(2,1)} %cen.1, s32[1,128]{1,0:T(1,128)} %bitcast.4, s32[1,32]{1,0:T(1,128)} %order_in.1, s32[1,32]{1,0:T(1,128)} %bitcast.5, s32[1]{0:T(128)S(6)} %copy.9.live), custom_call_target="tpu_custom_call" | custom-call | tf_op jit(solution)/shard_map/route/pallas_call | solution.py:266
  44.2 0.8 %copy.10 = bf16[24,9216]{1,0:T(8,128)(2,1)} copy(bf16[24,9216]{1,0:T(8,128)(2,1)S(1)} %bitcast.3) | data formatting | bytes 884736

commit v4 on v3

--- a/solution.py
+++ b/solution.py
@@ -39,9 +39,9 @@
     rank = zh * 8 + spot
 
     def ingest_peer(t):
-        n = t >> 2
-        dy = jnp.where((n & 1) == 0, 4 + (n >> 1), 3 - (n >> 1))
-        return (((g >> 2) + dy) & 7) * 4 + ((g & 3) ^ (3 - (t & 3)))
+        n = t & 7
+        dy = jnp.where((n & 1) == 0, 4 - (n >> 1), 5 + (n >> 1)) & 7
+        return (((g >> 2) + dy) & 7) * 4 + ((g & 3) ^ (3 - (t >> 3)))
 
     def owner(z, x_, c):
         return (x_ * 3 + z) * 2 + c
@@ -224,10 +224,10 @@
         @pl.loop(0, 8)
         def _(m):
             k = m >> 1
-            x_ = (xx + jnp.where(k < 2, k + 2, 3 - k)) & 3
+            x_ = (xx + jnp.where(k == 3, 0, jnp.where(k == 0, 2, 2 * k - 1))) & 3
             deliver(z, x_, core ^ (m & 1), jnp.where(m < ahead, 0, 1))
 
-    step = 1 + jnp.where((g & 3) < FIRST, 1, 0)
+    step = 1 + jnp.where((zh == 1) | ((zh == 0) & ((g & 3) < FIRST)), 1, 0)
     z0 = zh + step
     z0 = jnp.where(z0 >= 3, z0 - 3, z0)
     far(z0, AHEAD)

time: 45.1 us -> 44.7 us (level)
  the two profiles are of different devices: /device:TPU:1 before, /device:TPU:5 now
where the time goes in v4:
time: 44.7 us; the launch traced here: 44.5 us
  Pallas kernels  43.1 us (96%)
  local copies, waits for them, and re-layouts  0.76 us (2%)
  between operations  0.66 us (1%)
    pallas_call x1, Pallas kernels, body(): pl.pallas_call(kernel, out_shape=jax.ShapeDtypeStruct((OCT, 8, NI * WIDE)...  43.1 us

profile of v4, /device:TPU:5, one launch (start us, length us, event | category | flops | bytes accessed | tf_op | source)
XLA Modules:
  0.0 44.5 jit_solution(9588084955741706602)
XLA Ops:
  0.7 43.1 %route.1 = bf16[3,8,9216]{2,1,0:T(8,128)(2,1)S(1)} custom-call(bf16[128,768]{1,0:T(8,128)(2,1)} %vec.1, bf16[768,768]{1,0:T(8,128)(2,1)} %rot.1, bf16[64,768]{1,0:T(8,128)(2,1)} %cen.1, s32[1,128]{1,0:T(1,128)} %bitcast.4, s32[1,32]{1,0:T(1,128)} %order_in.1, s32[1,32]{1,0:T(1,128)} %bitcast.5, s32[1]{0:T(128)S(6)} %copy.9.live), custom_call_target="tpu_custom_call" | custom-call | tf_op jit(solution)/shard_map/route/pallas_call | solution.py:266
  43.8 0.8 %copy.10 = bf16[24,9216]{1,0:T(8,128)(2,1)} copy(bf16[24,9216]{1,0:T(8,128)(2,1)S(1)} %bitcast.3) | data formatting | bytes 884736

commit v5 on v4

--- a/solution.py
+++ b/solution.py
@@ -178,7 +178,7 @@
     def look(half, first):
         table = [[tbl[half, quad, f].astype(f32) for f in range(OCT)] for quad in range(QUADS)]
 
-        @pl.loop(0, NG, unroll=16)
+        @pl.loop(0, NG, unroll=32)
         def _(b):
             lane0 = jnp.broadcast_to(pos[pl.ds(b, 1)], (8, 128))
             want = jnp.broadcast_to(grp[pl.ds(b, 1)], (8, 128)) - half * QUADS
@@ -232,6 +232,8 @@
     z0 = jnp.where(z0 >= 3, z0 - 3, z0)
     far(z0, AHEAD)
 
+    far(3 - zh - z0, 0)
+
     @pl.when(spot < 7)
     def _():
         pl.semaphore_wait(entered.at[zh], 7 - spot)
@@ -240,7 +242,6 @@
     def _(m):
         deliver(zh, (xx + (m >> 1)) & 3, core ^ (m & 1), 1)
 
-    far(3 - zh - z0, 0)
 
     pack(i)
     own = pltpu.make_async_copy(send2.at[i], out.at[:, :, columns], lsem.at[7])

time: 44.7 us -> 44.4 us (level)
  the two profiles are of different devices: /device:TPU:5 before, /device:TPU:1 now
where the time goes in v5:
time: 44.4 us; the launch traced here: 43.6 us
  Pallas kernels  42.2 us (95%)
  local copies, waits for them, and re-layouts  0.76 us (2%)
  between operations  0.66 us (1%)
    pallas_call x1, Pallas kernels, body(): pl.pallas_call(kernel, out_shape=jax.ShapeDtypeStruct((OCT, 8, NI * WIDE)...  42.2 us

profile of v5, /device:TPU:1, one launch (start us, length us, event | category | flops | bytes accessed | tf_op | source)
XLA Modules:
  0.0 43.6 jit_solution(340395571369924732)
XLA Ops:
  0.7 42.2 %route.1 = bf16[3,8,9216]{2,1,0:T(8,128)(2,1)S(1)} custom-call(bf16[128,768]{1,0:T(8,128)(2,1)} %vec.1, bf16[768,768]{1,0:T(8,128)(2,1)} %rot.1, bf16[64,768]{1,0:T(8,128)(2,1)} %cen.1, s32[1,128]{1,0:T(1,128)} %bitcast.4, s32[1,32]{1,0:T(1,128)} %order_in.1, s32[1,32]{1,0:T(1,128)} %bitcast.5, s32[1]{0:T(128)S(6)} %copy.9.live), custom_call_target="tpu_custom_call" | custom-call | tf_op jit(solution)/shard_map/route/pallas_call | solution.py:267
  42.9 0.8 %copy.10 = bf16[24,9216]{1,0:T(8,128)(2,1)} copy(bf16[24,9216]{1,0:T(8,128)(2,1)S(1)} %bitcast.3) | data formatting | bytes 884736
